TPU v7x, 32 devices: a whole 2x2x4 slice. The times are simulated.
32 devices in a mesh: ens: 2 (over x), lon: 16 (over z, y, core).
Axes of the slice: x: 2, y: 2, z: 4, core: 2. Of those that a mesh axis runs over, the one named last changes fastest.
Arguments:
- increment: float32 [4, 4, 128, 512], P(None, None, ('ens', 'lon')), parts along dimension 2, may hold values from -12 to 12
- coeffs: float32 [3, 4, 128, 512], P(None, None, ('ens', 'lon')), parts along dimension 2, may hold values from 0.02 to 0.3
- polar_rows: int32 [64], P('ens'), parts along dimension 0, may hold values from 0 to 511, as said below
- polar_weight: float32 [64], P('ens'), parts along dimension 0, may hold values from 0.2 to 0.8
- block_index: int32 [512], P(('ens', 'lon')), parts along dimension 0, may hold values from 0 to 63
- send_dest: int32 [512], P(('ens', 'lon')), parts along dimension 0, may hold values from 0 to 15, as said below
- slot_count: int32 [512], P(('ens', 'lon')), parts along dimension 0, may hold values from 0 to 2, as said below
- jacobian: float32 [1024, 8, 512], P(('ens', 'lon')), parts along dimension 0, may hold values from -2 to 2
- observed: float32 [1024, 8], P(('ens', 'lon')), parts along dimension 0, may hold values from -6 to 6
- obs_weight: float32 [1024, 8], P(('ens', 'lon')), parts along dimension 0, may hold values from 0.25 to 4
- bg_weight: float32 [4, 4], replicated, may hold values from 0.02 to 0.1
Outputs:
- gradient: float32 [4, 4, 128, 512], P(None, None, ('ens', 'lon')), parts along dimension 2
- model_state: float32 [4, 4, 128, 512], P(None, None, ('ens', 'lon')), parts along dimension 2
- obs_residual: float32 [1024, 8], P(('ens', 'lon')), parts along dimension 0
There are 2 independent parts, one for each index of `ens`. A program takes and returns all parts, laid end to end along the dimension named above; an argument that names none is the same for every part. Nothing has to cross between parts.
Inputs may be any that keep to these rules, and one draw needn't show every extreme that they name: `polar_rows`: 32 distinct latitudes, half among the 32 lowest and half among the 32 highest. `send_dest`: each device sends exactly 16 blocks and at most 2 to one owner; some owner receives 2 from every device. `slot_count`: entry o * 16 + s counts the sends of device s to owner o.
All inputs are finite; a program needn't handle non-finite values.
Results may differ from a plain program's by a relative error of at most 0.0001.
Values sent between devices are 32-bit elements; how exact they have to be, the bound alone decides.
A program may use at most 128 MiB of HBM per device.

v0:
```python
import jax
import jax.numpy as jnp
from jax import lax
from jax.sharding import PartitionSpec as P

STEPS = 4
CAP = 2


def shifted(block, axis, distance):
    devices = range(lax.axis_size(axis))
    route = [((i - distance) % len(devices), i) for i in devices]
    return lax.ppermute(block, axis, route)


def advance_local(padded, coeffs):
    west_c, north_c, south_c = (coeffs[0], coeffs[1], coeffs[2])
    centre = padded[:, :, 1:]
    west_cells = padded[:, :, :-1]
    zero_edge = jnp.zeros_like(centre[..., :1])
    north_cells = jnp.concatenate([centre[..., 1:], zero_edge], axis=3)
    south_cells = jnp.concatenate([zero_edge, centre[..., :-1]], axis=3)
    return (
        (1.0 - west_c - north_c - south_c) * centre
        + west_c * west_cells
        + north_c * north_cells
        + south_c * south_cells
    )


def polar_blend(field_in, polar_rows, polar_weight, columns):
    polar_vals = field_in[..., polar_rows]
    partial_value = jnp.sum(polar_vals, axis=2)
    zonal_sum = lax.psum(partial_value, "lon")
    zonal_mean = zonal_sum / (columns * lax.axis_size("lon"))
    blended = (1.0 - polar_weight) * polar_vals + polar_weight * zonal_mean[:, :, None, :]
    return field_in.at[..., polar_rows].set(blended)


def retreat_local(adjoint_in, coeffs):
    west_c, north_c, south_c = (coeffs[0], coeffs[1], coeffs[2])
    east_flux = west_c * adjoint_in
    east_edge = shifted(east_flux[:, :, :1], "lon", -1)
    from_east = jnp.concatenate([east_flux[:, :, 1:], east_edge], axis=2)
    zero_edge = jnp.zeros_like(adjoint_in[..., :1])
    north_flux = north_c * adjoint_in
    south_flux = south_c * adjoint_in
    north_in = jnp.concatenate([zero_edge, north_flux[..., :-1]], axis=3)
    south_in = jnp.concatenate([south_flux[..., 1:], zero_edge], axis=3)
    return (1.0 - west_c - north_c - south_c) * adjoint_in + from_east + north_in + south_in


def shards(
    increment,
    coeffs,
    polar_rows,
    polar_weight,
    block_index,
    send_dest,
    slot_count,
    jacobian,
    observed,
    obs_weight,
    bg_weight,
):
    columns = increment.shape[2]
    lat_cells = increment.shape[3]
    device_count = lax.axis_size("lon")
    model_state = increment
    for repeat in range(STEPS):
        west_edge = shifted(model_state[:, :, -1:], "lon", 1)
        padded = jnp.concatenate([west_edge, model_state], axis=2)
        model_state = polar_blend(advance_local(padded, coeffs), polar_rows, polar_weight, columns)
    blocks = model_state.reshape(-1, lat_cells)
    sent_blocks = blocks[block_index]
    same_dest = send_dest[:, None] == send_dest[None, :]
    position = jnp.arange(send_dest.shape[0], dtype=jnp.int32)
    earlier = position[None, :] < position[:, None]
    rank_in = jnp.sum((same_dest & earlier).astype(jnp.int32), axis=1)
    slot_row = send_dest * CAP + rank_in
    outgoing = jnp.zeros((device_count * CAP, lat_cells), jnp.float32).at[slot_row].set(sent_blocks)
    received = lax.all_to_all(outgoing, "lon", split_axis=0, concat_axis=0, tiled=True)
    model_obs = jnp.einsum("soc,sc->so", jacobian, received, precision=lax.Precision.HIGHEST)
    live_mask = (
        (jnp.arange(CAP, dtype=jnp.int32)[None, :] < slot_count[:, None])
        .astype(jnp.float32)
        .reshape(-1, 1)
    )
    weighted = obs_weight * live_mask
    misfit = model_obs - observed
    bias_term = jnp.sum(weighted * misfit) / (1.0 + jnp.sum(weighted))
    residual = weighted * (misfit - bias_term)
    returned = jnp.einsum("soc,so->sc", jacobian, residual, precision=lax.Precision.HIGHEST)
    returned_rows = lax.all_to_all(returned, "lon", split_axis=0, concat_axis=0, tiled=True)
    contrib = returned_rows[slot_row]
    adjoint = jnp.zeros_like(blocks).at[block_index].add(contrib).reshape(model_state.shape)
    for repeat in range(STEPS):
        adjoint = retreat_local(polar_blend(adjoint, polar_rows, polar_weight, columns), coeffs)
    gradient = bg_weight[:, :, None, None] * increment + adjoint
    return (gradient, model_state, residual)


def solution(mesh):
    placed = (
        P(None, None, ("ens", "lon"), None),
        P(None, None, ("ens", "lon"), None),
        P("ens"),
        P("ens"),
        P(("ens", "lon")),
        P(("ens", "lon")),
        P(("ens", "lon")),
        P(("ens", "lon"), None, None),
        P(("ens", "lon"), None),
        P(("ens", "lon"), None),
        P(),
    )
    return jax.shard_map(
        shards,
        mesh=mesh,
        in_specs=placed,
        out_specs=(
            P(None, None, ("ens", "lon"), None),
            P(None, None, ("ens", "lon"), None),
            P(("ens", "lon"), None),
        ),
        check_vma=False,
    )
```

profile of v0, /device:TPU:0, one launch (start us, length us, event | category | flops | bytes accessed | tf_op | source)
XLA Modules:
  0.0 853.9 jit_solution(2343139794600207057)
XLA Ops:
  19.7 7.3 multiply_add_fusion.3
  30.1 62.6 %psum.56 = f32[4,4,32]{1,0,2:T(4,128)S(1)} all-reduce(f32[4,4,32]{1,0,2:T(4,128)S(1)} %bitcast_reduce_fusion.7), channel_id=1, replica_groups=mesh['ens'=2,'lon'=16] {'lon'}, use_global_device_ids=true, to_apply=%region_2.0 | all-reduce | flops 512 | bytes 4096 | tf_op jit(solution)/shard_map/psum | solution.py:34
  96.9 6.5 slice.182
  126.1 7.3 multiply_add_fusion.2
  136.5 62.4 %psum.57 = f32[4,4,32]{1,0,2:T(4,128)S(1)} all-reduce(f32[4,4,32]{1,0,2:T(4,128)S(1)} %bitcast_reduce_fusion.6), channel_id=1, replica_groups=mesh['ens'=2,'lon'=16] {'lon'}, use_global_device_ids=true, to_apply=%region_5.0 | all-reduce | flops 512 | bytes 4096 | tf_op jit(solution)/shard_map/psum | solution.py:34
  203.1 6.5 slice.185
  232.3 7.3 multiply_add_fusion.1
  242.7 62.0 %psum.58 = f32[4,4,32]{1,0,2:T(4,128)S(1)} all-reduce(f32[4,4,32]{1,0,2:T(4,128)S(1)} %bitcast_reduce_fusion.5), channel_id=1, replica_groups=mesh['ens'=2,'lon'=16] {'lon'}, use_global_device_ids=true, to_apply=%region_8.0 | all-reduce | flops 512 | bytes 4096 | tf_op jit(solution)/shard_map/psum | solution.py:34
  308.9 6.5 slice.188
  338.5 7.3 multiply_add_fusion
  349.0 62.0 %psum.59 = f32[4,4,32]{1,0,2:T(4,128)S(1)} all-reduce(f32[4,4,32]{1,0,2:T(4,128)S(1)} %bitcast_reduce_fusion.4), channel_id=1, replica_groups=mesh['ens'=2,'lon'=16] {'lon'}, use_global_device_ids=true, to_apply=%region_11.0 | all-reduce | flops 512 | bytes 4096 | tf_op jit(solution)/shard_map/psum | solution.py:34
  423.9 6.7 all-to-all-done
  452.8 61.9 %psum.60 = f32[4,4,32]{1,0,2:T(4,128)S(1)} all-reduce(f32[4,4,32]{1,0,2:T(4,128)S(1)} %bitcast_reduce_fusion.3), channel_id=1, replica_groups=mesh['ens'=2,'lon'=16] {'lon'}, use_global_device_ids=true, to_apply=%region_18.0 | all-reduce | flops 512 | bytes 4096 | tf_op jit(solution)/shard_map/psum | solution.py:34
  527.2 7.0 slice_multiply_fusion.7
  541.6 10.3 %fusion.1 = f32[4,4,4,512]{2,1,3,0:T(4,128)} fusion(f32[4,4,1,512]{2,1,3,0:T(4,128)} %copy.146, f32[4,4,3,512]{2,1,3,0:T(4,128)} %slice.191, f32[4,4,4,511]{2,1,3,0:T(4,128)} %get-tuple-element.27, f32[4,4,4,511]{2,1,3,0:T(4,128)} %get-tuple-element.26, f32[4,4,4,512]{2,1,3,0:T(4,128)} %scatter_fusion.4, f32[4,4,512]{1,0,2:T(4,128)S(1)} %copy.115), kind=kLoop, calls=%fused_computation.22 | loop fusion | flops 163840 | bytes 687616 | tf_op jit(solution)/shard_map/add | solution.py:50
  555.1 58.0 %psum.61 = f32[4,4,32]{1,0,2:T(4,128)S(1)} all-reduce(f32[4,4,32]{1,0,2:T(4,128)S(1)} %bitcast_reduce_fusion.2), channel_id=1, replica_groups=mesh['ens'=2,'lon'=16] {'lon'}, use_global_device_ids=true, to_apply=%region_21.0 | all-reduce | flops 512 | bytes 4096 | tf_op jit(solution)/shard_map/psum | solution.py:34
  625.6 7.0 slice_multiply_fusion.5
  639.9 10.4 %fusion.3 = f32[4,4,4,512]{2,1,3,0:T(4,128)} fusion(f32[4,4,1,512]{2,1,3,0:T(4,128)} %copy.148, f32[4,4,3,512]{2,1,3,0:T(4,128)} %slice.197, f32[4,4,4,511]{2,1,3,0:T(4,128)} %get-tuple-element.25, f32[4,4,4,511]{2,1,3,0:T(4,128)} %get-tuple-element.24, f32[4,4,4,512]{2,1,3,0:T(4,128)} %scatter_fusion.5, f32[4,4,512]{1,0,2:T(4,128)S(1)} %copy.115), kind=kLoop, calls=%fused_computation.25 | loop fusion | flops 163840 | bytes 687616 | tf_op jit(solution)/shard_map/add | solution.py:50
  653.5 58.0 %psum.62 = f32[4,4,32]{1,0,2:T(4,128)S(1)} all-reduce(f32[4,4,32]{1,0,2:T(4,128)S(1)} %bitcast_reduce_fusion.1), channel_id=1, replica_groups=mesh['ens'=2,'lon'=16] {'lon'}, use_global_device_ids=true, to_apply=%region_24.0 | all-reduce | flops 512 | bytes 4096 | tf_op jit(solution)/shard_map/psum | solution.py:34
  723.9 7.0 slice_multiply_fusion.3
  738.3 10.3 %fusion.5 = f32[4,4,4,512]{2,1,3,0:T(4,128)} fusion(f32[4,4,1,512]{2,1,3,0:T(4,128)} %copy.150, f32[4,4,3,512]{2,1,3,0:T(4,128)} %slice.203, f32[4,4,4,511]{2,1,3,0:T(4,128)} %get-tuple-element.23, f32[4,4,4,511]{2,1,3,0:T(4,128)} %get-tuple-element.22, f32[4,4,4,512]{2,1,3,0:T(4,128)} %scatter_fusion.6, f32[4,4,512]{1,0,2:T(4,128)S(1)} %copy.115), kind=kLoop, calls=%fused_computation.28 | loop fusion | flops 163840 | bytes 687616 | tf_op jit(solution)/shard_map/add | solution.py:50
  751.8 57.9 %psum.63 = f32[4,4,32]{1,0,2:T(4,128)S(1)} all-reduce(f32[4,4,32]{1,0,2:T(4,128)S(1)} %bitcast_reduce_fusion), channel_id=1, replica_groups=mesh['ens'=2,'lon'=16] {'lon'}, use_global_device_ids=true, to_apply=%region_27.0 | all-reduce | flops 512 | bytes 4096 | tf_op jit(solution)/shard_map/psum | solution.py:34
  822.4 6.8 slice_multiply_fusion.1
  836.5 12.5 %fusion.8 = f32[4,4,4,512]{2,1,3,0:T(4,128)} fusion(f32[4,4,4,512]{2,1,3,0:T(4,128)} %copy.153, f32[4,4,1,512]{2,1,3,0:T(4,128)} %copy.152, f32[4,4,3,512]{2,1,3,0:T(4,128)} %slice.209, f32[4,4,4,511]{2,1,3,0:T(4,128)} %get-tuple-element.21, f32[4,4,4,511]{2,1,3,0:T(4,128)} %get-tuple-element.20, f32[4,4,4,512]{2,1,3,0:T(4,128)} %scatter_fusion.7, ...), kind=kLoop, calls=%fused_computation.32 | loop fusion | flops 196608 | bytes 818688 | tf_op jit(solution)/shard_map/add | solution.py:99
  (175 shorter events, 239.4 us)
Async XLA Ops:
  0.6 430.1 %copy-start = (f32[32,8,512]{2,1,0:T(8,128)S(1)}, f32[32,8,512]{2,1,0:T(8,128)}, u32[]{:S(2)}) copy-start(f32[32,8,512]{2,1,0:T(8,128)} %param.18) | copy-start | bytes 1572868
  1.7 14.7 %collective-permute-start = (f32[4,4,1,512]{3,1,2,0:T(4,128)S(1)}, f32[4,4,1,512]{3,1,2,0:T(4,128)S(1)}, u32[]{:S(2)}, u32[]{:S(2)}) collective-permute-start(f32[4,4,1,512]{3,1,2,0:T(4,128)S(1)} %slice.181), channel_id=1, source_target_pairs={{15,0},{0,1},{1,2},{2,3},{3,4},{4,5},{5,6},{6,7},{7,8},{8,9},{9,10... | collective-permute-start | bytes 98312 | tf_op jit(solution)/shard_map/ppermute | solution.py:13
  9.5 6.9 copy-start.10
  9.5 6.9 copy-start.15
  111.2 11.6 %collective-permute-start.1 = (f32[4,4,1,512]{3,1,2,0:T(4,128)S(1)}, f32[4,4,1,512]{3,1,2,0:T(4,128)S(1)}, u32[]{:S(2)}, u32[]{:S(2)}) collective-permute-start(f32[4,4,1,512]{3,1,2,0:T(4,128)S(1)} %copy.127), channel_id=1, source_target_pairs={{15,0},{0,1},{1,2},{2,3},{3,4},{4,5},{5,6},{6,7},{7,8},{8,9},{9,10... | collective-permute-start | bytes 98312 | tf_op jit(solution)/shard_map/ppermute | solution.py:13
  203.1 6.5 copy-start.3
  217.5 11.6 %collective-permute-start.2 = (f32[4,4,1,512]{3,1,2,0:T(4,128)S(1)}, f32[4,4,1,512]{3,1,2,0:T(4,128)S(1)}, u32[]{:S(2)}, u32[]{:S(2)}) collective-permute-start(f32[4,4,1,512]{3,1,2,0:T(4,128)S(1)} %copy.132), channel_id=1, source_target_pairs={{15,0},{0,1},{1,2},{2,3},{3,4},{4,5},{5,6},{6,7},{7,8},{8,9},{9,10... | collective-permute-start | bytes 98312 | tf_op jit(solution)/shard_map/ppermute | solution.py:13
  323.3 12.0 %collective-permute-start.3 = (f32[4,4,1,512]{3,1,2,0:T(4,128)S(1)}, f32[4,4,1,512]{3,1,2,0:T(4,128)S(1)}, u32[]{:S(2)}, u32[]{:S(2)}) collective-permute-start(f32[4,4,1,512]{3,1,2,0:T(4,128)S(1)} %copy.137), channel_id=1, source_target_pairs={{15,0},{0,1},{1,2},{2,3},{3,4},{4,5},{5,6},{6,7},{7,8},{8,9},{9,10... | collective-permute-start | bytes 98312 | tf_op jit(solution)/shard_map/ppermute | solution.py:13
  345.8 78.0 %copy-start.16 = (s32[16]{0:T(128)S(1)}, s32[16]{0:T(128)}, u32[]{:S(2)}) copy-start(s32[16]{0:T(128)} %param.17) | copy-start | bytes 196
  345.8 86.1 %copy-start.12 = (f32[32,8]{0,1:T(8,128)S(1)}, f32[32,8]{0,1:T(8,128)}, u32[]{:S(2)}) copy-start(f32[32,8]{0,1:T(8,128)} %param.20) | copy-start | bytes 3076
  345.8 86.1 %copy-start.13 = (f32[32,8]{0,1:T(8,128)S(1)}, f32[32,8]{0,1:T(8,128)}, u32[]{:S(2)}) copy-start(f32[32,8]{0,1:T(8,128)} %param.19) | copy-start | bytes 3076
  418.7 26.9 %copy-start.11 = (f32[4,4,4,512]{3,2,1,0:T(4,128)}, f32[4,4,4,512]{3,2,1,0:T(4,128)S(1)}, u32[]{:S(2)}) copy-start(f32[4,4,4,512]{3,2,1,0:T(4,128)S(1)} %copy.142) | copy-start | bytes 393220
  420.2 10.4 %all-to-all-start = ((f32[16,2,512]{2,1,0:T(2,128)}), f32[16,2,512]{2,1,0:T(2,128)S(1)}, u32[]{:S(2)}, u32[]{:S(2)}) async-start(f32[16,2,512]{2,1,0:T(2,128)} %all_to_all.16), calls=%async_computation | async-start | bytes 131072 | tf_op jit(solution)/shard_map/all_to_all | solution.py:82
  433.8 11.8 %copy-start.14 = (f32[32,8]{0,1:T(8,128)}, f32[32,8]{0,1:T(8,128)S(1)}, u32[]{:S(2)}) copy-start(f32[32,8]{0,1:T(8,128)S(1)} %subtract_multiply_fusion) | copy-start | bytes 3076
  435.1 10.5 %all-to-all-start.1 = ((f32[16,2,512]{2,1,0:T(2,128)}), f32[16,2,512]{2,1,0:T(2,128)S(1)}, u32[]{:S(2)}, u32[]{:S(2)}) async-start(f32[16,2,512]{2,1,0:T(2,128)} %all_to_all.19), calls=%async_computation.1 | async-start | bytes 131072 | tf_op jit(solution)/shard_map/all_to_all | solution.py:94
  527.0 7.2 copy-start.6
  527.0 11.4 %collective-permute-start.4 = (f32[4,4,1,512]{3,1,2,0:T(4,128)S(1)}, f32[4,4,1,512]{3,1,2,0:T(4,128)S(1)}, u32[]{:S(2)}, u32[]{:S(2)}) collective-permute-start(f32[4,4,1,512]{3,1,2,0:T(4,128)S(1)} %copy.162), channel_id=1, source_target_pairs={{1,0},{2,1},{3,2},{4,3},{5,4},{6,5},{7,6},{8,7},{9,8},{10,9},{11,1... | collective-permute-start | bytes 98312 | tf_op jit(solution)/shard_map/ppermute | solution.py:13
  625.3 7.3 copy-start.7
  625.3 11.4 %collective-permute-start.5 = (f32[4,4,1,512]{3,1,2,0:T(4,128)S(1)}, f32[4,4,1,512]{3,1,2,0:T(4,128)S(1)}, u32[]{:S(2)}, u32[]{:S(2)}) collective-permute-start(f32[4,4,1,512]{3,1,2,0:T(4,128)S(1)} %copy.163), channel_id=1, source_target_pairs={{1,0},{2,1},{3,2},{4,3},{5,4},{6,5},{7,6},{8,7},{9,8},{10,9},{11,1... | collective-permute-start | bytes 98312 | tf_op jit(solution)/shard_map/ppermute | solution.py:13
  723.6 7.3 copy-start.8
  723.6 11.5 %collective-permute-start.6 = (f32[4,4,1,512]{3,1,2,0:T(4,128)S(1)}, f32[4,4,1,512]{3,1,2,0:T(4,128)S(1)}, u32[]{:S(2)}, u32[]{:S(2)}) collective-permute-start(f32[4,4,1,512]{3,1,2,0:T(4,128)S(1)} %copy.164), channel_id=1, source_target_pairs={{1,0},{2,1},{3,2},{4,3},{5,4},{6,5},{7,6},{8,7},{9,8},{10,9},{11,1... | collective-permute-start | bytes 98312 | tf_op jit(solution)/shard_map/ppermute | solution.py:13
  822.0 7.2 copy-start.5
  822.0 11.4 %collective-permute-start.7 = (f32[4,4,1,512]{3,1,2,0:T(4,128)S(1)}, f32[4,4,1,512]{3,1,2,0:T(4,128)S(1)}, u32[]{:S(2)}, u32[]{:S(2)}) collective-permute-start(f32[4,4,1,512]{3,1,2,0:T(4,128)S(1)} %copy.165), channel_id=1, source_target_pairs={{1,0},{2,1},{3,2},{4,3},{5,4},{6,5},{7,6},{8,7},{9,8},{10,9},{11,1... | collective-permute-start | bytes 98312 | tf_op jit(solution)/shard_map/ppermute | solution.py:13
  836.5 16.9 %copy-start.1 = (f32[32,8,512]{2,1,0:T(8,128)S(1)}, f32[32,8,512]{2,1,0:T(8,128)}, u32[]{:S(2)}) copy-start(f32[32,8,512]{2,1,0:T(8,128)} %param.18) | copy-start | bytes 1572868
  (3 other events, 17.1 us)
where the time goes:
time: 864 us; the launch traced here: 854 us
  blocking collectives  485 us (56%)
  local copies, waits for them, and re-layouts  206 us (24%)
  other arithmetic  143 us (17%)
  starting transfers between devices  9.22 us (1%)
    psum x8, blocking collectives, polar_blend(): zonal_sum = lax.psum(partial_value, 'lon')  485 us
    scatter x12, local copies, waits for them, and re-layouts, polar_blend(): return field_in.at[..., polar_rows].set(blended)  44.9 us
    add x3, other arithmetic, retreat_local(): (1.0 - west_c - north_c - south_c) * adjoint_in + from_east + north_in  31 us
    slice x7, local copies, waits for them, and re-layouts, shards(): west_edge = shifted(model_state[:, :, -1:], 'lon', 1)  30.2 us
    add x8, other arithmetic, advance_local(): (1.0 - west_c - north_c - south_c) * centre + west_c * west_cells  29.3 us
    mul x4, other arithmetic, retreat_local(): north_flux = north_c * adjoint_in  27.8 us
    unnamed x43, local copies, waits for them, and re-layouts  26.1 us
    gather x8, local copies, waits for them, and re-layouts, polar_blend(): polar_vals = field_in[..., polar_rows]  23.5 us
  transfers between devices with their start and end apart: 10, of which 1 were waited for; matrix products, arithmetic and copies ran while one was open for 12% of the time, Pallas kernels for 0%

commit v1 on v0

v1 whole, which is shorter than its diff:
```python
import functools

import jax
import jax.numpy as jnp
from jax import lax
from jax.experimental import pallas as pl
from jax.experimental.pallas import tpu as pltpu
from jax.sharding import PartitionSpec as P

STEPS = 4
CAP = 2
LANES = 128
HALF = 64
MESH = pl.DeviceIdType.MESH
EXACT = lax.Precision.HIGHEST


def kernel(
    n,
    sizes,
    x_ref,
    c_ref,
    rows_ref,
    pw_ref,
    bi_ref,
    sd_ref,
    sc_ref,
    jac_hbm,
    obs_ref,
    ow_ref,
    bg_ref,
    grad_ref,
    ms_ref,
    res_ref,
    jac,
    xarr,
    xwest,
    cwest,
    ceast,
    coef,
    msg,
    pbuf,
    pcoef,
    mout,
    mbuf,
    xfin,
    blk_out,
    blk_in,
    ret_out,
    ret_in,
    garr,
    geast,
    gmsg,
    gbuf,
    amout,
    ambuf,
    send_sem,
    recv_sem,
    jac_sem,
):
    tl, cols, lat, levels, sends, poles, obs = sizes
    solvers = tl
    me = lax.axis_index("lon")
    east, west = lax.rem(me + 1, n), lax.rem(me + n - 1, n)

    def others(count, act):
        if count == n:
            def body(s, carry):
                act(lax.rem(me + s, n))
                return carry

            lax.fori_loop(1, n, body, 0)
        else:
            def body(j, carry):
                @pl.when(j != me)
                def _():
                    act(j)

                return carry

            lax.fori_loop(0, count, body, 0)

    def remote(src, dst, phase, device):
        return pltpu.make_async_remote_copy(
            src_ref=src,
            dst_ref=dst,
            send_sem=send_sem.at[phase],
            recv_sem=recv_sem.at[phase],
            device_id={"lon": device},
            device_id_type=MESH,
        )

    def wait_bytes(ref, sem):
        pltpu.make_async_copy(ref, ref, sem).wait()

    def is_solver():
        return me < solvers

    def when_solver(act):
        if solvers == n:
            act()
        else:
            pl.when(is_solver())(act)

    def wait_solver_sends(ref, sem):
        if solvers == n:
            wait_bytes(ref.at[pl.ds(0, n - 1)], sem)
        else:
            @pl.when(is_solver())
            def _():
                wait_bytes(ref.at[pl.ds(0, solvers - 1)], sem)

            @pl.when(jnp.logical_not(is_solver()))
            def _():
                wait_bytes(ref.at[pl.ds(0, solvers)], sem)

    jac_copy = pltpu.make_async_copy(jac_hbm, jac, jac_sem)
    jac_copy.start()

    barrier = pltpu.get_barrier_semaphore()
    others(
        n,
        lambda j: pl.semaphore_signal(
            barrier, inc=1, device_id={"lon": j}, device_id_type=MESH
        ),
    )

    lane = lax.broadcasted_iota(jnp.int32, (1, LANES), 1)
    south = lane < HALF

    def pack(first, last):
        return jnp.where(south, first, last)

    msg[:, 0:cols, :] = pack(x_ref[:, :, 0:LANES], x_ref[:, :, lat - LANES : lat])
    for kind in range(3):
        part = pack(c_ref[kind, :, :, 0:LANES], c_ref[kind, :, :, lat - LANES : lat])
        lo = cols * (kind + 1)
        for t in range(tl // levels):
            msg[t * levels : (t + 1) * levels, lo : lo + cols, :] = part

    pl.semaphore_wait(barrier, n - 1)
    others(solvers, lambda j: remote(msg.at[j], pbuf.at[me], 0, j).start())

    for c in range(cols):
        xarr[c * tl : (c + 1) * tl, :] = x_ref[:, c, :]
    to_east = remote(xarr, xwest, 6, east)
    to_east.start()
    coef_east = remote(c_ref, cwest, 7, east)
    coef_east.start()
    coef_west = remote(c_ref, ceast, 8, west)
    coef_west.start()

    when_solver(lambda: pbuf.__setitem__((pl.ds(me, 1),), msg[pl.ds(me, 1)]))

    lat_row = lax.broadcasted_iota(jnp.int32, (1, lat), 1)
    weight = jnp.zeros((1, lat), jnp.float32)
    for p in range(poles):
        weight = jnp.where(lat_row == rows_ref[p], pw_ref[p], weight)
    w_first, w_last = weight[:, 0:LANES], weight[:, lat - LANES : lat]
    w_pack = pack(w_first, w_last)
    keep_pack = 1.0 - w_pack

    def edge_free(cn, cs, row, last):
        return jnp.where(row == last, 0.0, cn), jnp.where(row == 0, 0.0, cs)

    def arrange(src, base):
        for c in range(cols):
            cw, cn, cs = src[0, :, c, :], src[1, :, c, :], src[2, :, c, :]
            centre = 1.0 - cw - cn - cs
            cn, cs = edge_free(cn, cs, lat_row, lat - 1)
            for kind, value in enumerate((centre, cw, cn, cs)):
                coef[base + c, kind] = jnp.concatenate([value, value], axis=0)

    arrange(c_ref, cols)

    def routing(shape, owner_axis):
        owner = lax.broadcasted_iota(jnp.int32, shape, owner_axis)
        block = lax.broadcasted_iota(jnp.int32, shape, 1 - owner_axis)

        def body(k, carry):
            seen, first, second = carry
            index = bi_ref[k]
            row = lax.rem(index, cols) * tl + lax.div(index, cols)
            to_owner = owner == sd_ref[k]
            here = jnp.logical_and(to_owner, block == row)
            first = jnp.where(jnp.logical_and(here, seen == 0), 1.0, first)
            second = jnp.where(jnp.logical_and(here, seen == 1), 1.0, second)
            return jnp.where(to_owner, seen + 1, seen), first, second

        zero = jnp.zeros(shape, jnp.float32)
        init = (jnp.zeros(shape, jnp.int32), zero, zero)
        return lax.fori_loop(0, sends, body, init, unroll=sends <= 16)[1:]

    scatter_hot = routing((cols * tl, n), 1)
    gather_hot = routing((n, cols * tl), 0)

    eye = (
        lax.broadcasted_iota(jnp.int32, (obs, obs), 0)
        == lax.broadcasted_iota(jnp.int32, (obs, obs), 1)
    ).astype(jnp.float32)[None]
    slot_row = lax.broadcasted_iota(jnp.int32, (CAP * n, obs), 0)

    def live_body(d, live):
        mine = lax.div(slot_row, CAP) == d
        on = (lax.rem(slot_row, CAP) < sc_ref[d]).astype(jnp.float32)
        return jnp.where(mine, on, live)

    live = lax.fori_loop(
        0, n, live_body, jnp.zeros((CAP * n, obs), jnp.float32), unroll=n <= 16
    )

    def upright(flat):
        return jnp.sum(flat[:, None, :] * eye, axis=2, keepdims=True)

    weighted = upright(ow_ref[...] * live)
    observed = upright(obs_ref[...])
    weight_sum = 1.0 + jnp.sum(weighted, axis=(0, 1), keepdims=True)

    def solve_forward():
        wait_bytes(pbuf.at[pl.ds(0, n - 1)], recv_sem.at[0])
        v = [pbuf[:, c, :] for c in range(cols)]
        packs = []
        for c in range(cols):
            cw, cn, cs = (pbuf[:, cols * (k + 1) + c, :] for k in range(3))
            centre = 1.0 - cw - cn - cs
            cn, cs = edge_free(cn, cs, lane, LANES - 1)
            packs.append((centre, cw, cn, cs))
            for kind, value in enumerate(packs[c]):
                pcoef[c, kind] = value
        for step in range(STEPS):
            new = []
            for c in range(cols):
                centre, cw, cn, cs = packs[c]
                from_west = pltpu.roll(v[cols - 1], 1, 0) if c == 0 else v[c - 1]
                new.append(
                    centre * v[c]
                    + cw * from_west
                    + cn * pltpu.roll(v[c], LANES - 1, 1)
                    + cs * pltpu.roll(v[c], 1, 1)
                )
            total = sum(new[1:], new[0])
            mean = jnp.sum(total, axis=0, keepdims=True) / (cols * n)
            mout[step : step + 1, :] = mean
            v = [keep_pack * value + w_pack * mean for value in new]
        mbuf[pl.ds(me, 1)] = mout[...][None]
        others(n, lambda j: remote(mout, mbuf.at[me], 1, j).start())

    when_solver(solve_forward)

    coef_east.wait_recv()
    arrange(cwest, 0)
    coef_west.wait_recv()
    arrange(ceast, 2 * cols)
    to_east.wait_recv()
    wait_solver_sends(mbuf, recv_sem.at[1])

    def blend(value, first_mean, last_mean):
        middle = value[:, LANES : lat - LANES]
        first, last = value[:, 0:LANES], value[:, lat - LANES : lat]
        first = (1.0 - w_first) * first + w_first * first_mean
        last = (1.0 - w_last) * last + w_last * last_mean
        return jnp.concatenate([first, middle, last], axis=1)

    group = 2 * levels
    for h in range(tl // group):
        rows = slice(h * group, (h + 1) * group)
        at = lambda c: slice(c * tl + h * group, c * tl + (h + 1) * group)
        v = [xwest[at(c), :] for c in range(cols)] + [xarr[at(c), :] for c in range(cols)]
        for step in range(STEPS):
            mean = mbuf[rows, step, :]
            new = list(v)
            for c in range(step + 1, 2 * cols):
                value = (
                    coef[c, 0] * v[c]
                    + coef[c, 1] * v[c - 1]
                    + coef[c, 2] * pltpu.roll(v[c], lat - 1, 1)
                    + coef[c, 3] * pltpu.roll(v[c], 1, 1)
                )
                new[c] = blend(value, mean, mean)
            v = new
        for c in range(cols):
            xfin[at(c), :] = v[cols + c]
            ms_ref[rows, c, :] = v[cols + c]

    for r in range(CAP):
        blk_out[:, r, :] = jnp.dot(
            gather_hot[r], xfin[...], precision=EXACT, preferred_element_type=jnp.float32
        )
    others(n, lambda j: remote(blk_out.at[j], blk_in.at[me], 2, j).start())
    blk_in[pl.ds(me, 1)] = blk_out[pl.ds(me, 1)]
    jac_copy.wait()
    wait_bytes(blk_in.at[pl.ds(0, n - 1)], recv_sem.at[2])

    w4 = weighted.reshape(n, CAP, obs, 1)
    o4 = observed.reshape(n, CAP, obs, 1)
    misfit = []
    bias_sum = jnp.zeros((1, 1, 1), jnp.float32)
    for r in range(CAP):
        model = jnp.sum(jac[:, r] * blk_in[:, r : r + 1, :], axis=2, keepdims=True)
        misfit.append(model - o4[:, r])
        bias_sum += jnp.sum(w4[:, r] * misfit[r], axis=(0, 1), keepdims=True)
    bias = bias_sum / weight_sum
    residual = [w4[:, r] * (misfit[r] - bias) for r in range(CAP)]
    for r in range(CAP):
        ret_out[:, r : r + 1, :] = jnp.sum(jac[:, r] * residual[r], axis=1, keepdims=True)
    others(n, lambda j: remote(ret_out.at[j], ret_in.at[me], 3, j).start())
    ret_in[pl.ds(me, 1)] = ret_out[pl.ds(me, 1)]
    for r in range(CAP):
        res_ref[pl.ds(r, n, stride=CAP), :] = jnp.sum(residual[r] * eye, axis=1)
    wait_bytes(ret_in.at[pl.ds(0, n - 1)], recv_sem.at[3])

    start = jnp.dot(
        scatter_hot[0], ret_in[:, 0, :], precision=EXACT, preferred_element_type=jnp.float32
    )
    for r in range(1, CAP):
        start += jnp.dot(
            scatter_hot[r], ret_in[:, r, :], precision=EXACT, preferred_element_type=jnp.float32
        )
    garr[...] = start
    for c in range(cols):
        part = start[c * tl : (c + 1) * tl]
        gmsg[:, c, :] = pack(part[:, 0:LANES], part[:, lat - LANES : lat])
    others(solvers, lambda j: remote(gmsg.at[j], gbuf.at[me], 4, j).start())
    to_west = remote(garr, geast, 9, west)
    to_west.start()
    when_solver(lambda: gbuf.__setitem__((pl.ds(me, 1),), gmsg[pl.ds(me, 1)]))

    def solve_adjoint():
        wait_bytes(gbuf.at[pl.ds(0, n - 1)], recv_sem.at[4])
        g = [gbuf[:, c, :] for c in range(cols)]
        for step in range(STEPS):
            total = sum(g[1:], g[0])
            mean = jnp.sum(total, axis=0, keepdims=True) / (cols * n)
            amout[step : step + 1, :] = mean
            if step == STEPS - 1:
                break
            g = [keep_pack * value + w_pack * mean for value in g]
            flux = [pcoef[c, 1] * g[c] for c in range(cols)]
            new = []
            for c in range(cols):
                from_east = pltpu.roll(flux[0], n - 1, 0) if c == cols - 1 else flux[c + 1]
                new.append(
                    pcoef[c, 0] * g[c]
                    + from_east
                    + pltpu.roll(pcoef[c, 2] * g[c], 1, 1)
                    + pltpu.roll(pcoef[c, 3] * g[c], LANES - 1, 1)
                )
            g = new
        ambuf[pl.ds(me, 1)] = amout[...][None]
        others(n, lambda j: remote(amout, ambuf.at[me], 5, j).start())

    when_solver(solve_adjoint)
    to_west.wait_recv()
    wait_solver_sends(ambuf, recv_sem.at[5])

    group_row = lax.broadcasted_iota(jnp.int32, (group, 1), 0)
    for h in range(tl // group):
        rows = slice(h * group, (h + 1) * group)
        at = lambda c: slice(c * tl + h * group, c * tl + (h + 1) * group)
        g = [garr[at(c), :] for c in range(cols)] + [geast[at(c), :] for c in range(cols)]
        for step in range(STEPS):
            mean = ambuf[rows, step, :]
            last = 2 * cols - step
            g = [blend(value, mean, mean) for value in g[:last]]
            new = []
            for c in range(last - 1):
                k = cols + c
                new.append(
                    coef[k, 0] * g[c]
                    + coef[k + 1, 1] * g[c + 1]
                    + pltpu.roll(coef[k, 2] * g[c], 1, 1)
                    + pltpu.roll(coef[k, 3] * g[c], lat - 1, 1)
                )
            g = new
        background = jnp.zeros((group, 1), jnp.float32)
        for i in range(group):
            at_row = h * group + i
            value = bg_ref[at_row // levels, at_row % levels]
            background = jnp.where(group_row == i, value, background)
        for c in range(cols):
            grad_ref[rows, c, :] = background * xarr[at(c), :] + g[c]

    wait_solver_sends(msg, send_sem.at[0])
    wait_bytes(blk_out.at[pl.ds(0, n - 1)], send_sem.at[2])
    wait_bytes(ret_out.at[pl.ds(0, n - 1)], send_sem.at[3])
    wait_solver_sends(gmsg, send_sem.at[4])

    def drain_means():
        def body(s, carry):
            wait_bytes(mout, send_sem.at[1])
            wait_bytes(amout, send_sem.at[5])
            return carry

        lax.fori_loop(1, n, body, 0)

    when_solver(drain_means)
    to_east.wait_send()
    coef_east.wait_send()
    coef_west.wait_send()
    to_west.wait_send()


def shards(
    increment,
    coeffs,
    polar_rows,
    polar_weight,
    block_index,
    send_dest,
    slot_count,
    jacobian,
    observed,
    obs_weight,
    bg_weight,
):
    tracers, levels, cols, lat = increment.shape
    n = lax.axis_size("lon")
    tl = tracers * levels
    obs = jacobian.shape[1]
    sizes = (tl, cols, lat, levels, send_dest.shape[0], polar_rows.shape[0], obs)
    vmem = pl.BlockSpec(memory_space=pltpu.VMEM)
    smem = pl.BlockSpec(memory_space=pltpu.SMEM)
    f32 = jnp.float32
    field = jax.ShapeDtypeStruct((tl, cols, lat), f32)
    scratch = [
        pltpu.VMEM((n, CAP, obs, lat), f32),
        pltpu.VMEM((cols * tl, lat), f32),
        pltpu.VMEM((cols * tl, lat), f32),
        pltpu.VMEM(coeffs.shape, f32),
        pltpu.VMEM(coeffs.shape, f32),
        pltpu.VMEM((3 * cols, 4, 2 * levels, lat), f32),
        pltpu.VMEM((tl, 4 * cols, LANES), f32),
        pltpu.VMEM((n, 4 * cols, LANES), f32),
        pltpu.VMEM((cols, 4, n, LANES), f32),
        pltpu.VMEM((STEPS, LANES), f32),
        pltpu.VMEM((tl, STEPS, LANES), f32),
        pltpu.VMEM((cols * tl, lat), f32),
        pltpu.VMEM((n, CAP, lat), f32),
        pltpu.VMEM((n, CAP, lat), f32),
        pltpu.VMEM((n, CAP, lat), f32),
        pltpu.VMEM((n, CAP, lat), f32),
        pltpu.VMEM((cols * tl, lat), f32),
        pltpu.VMEM((cols * tl, lat), f32),
        pltpu.VMEM((tl, cols, LANES), f32),
        pltpu.VMEM((n, cols, LANES), f32),
        pltpu.VMEM((STEPS, LANES), f32),
        pltpu.VMEM((tl, STEPS, LANES), f32),
        pltpu.SemaphoreType.DMA((10,)),
        pltpu.SemaphoreType.DMA((10,)),
        pltpu.SemaphoreType.DMA,
    ]
    gradient, model_state, residual = pl.pallas_call(
        functools.partial(kernel, n, sizes),
        out_shape=(field, field, jax.ShapeDtypeStruct(observed.shape, f32)),
        in_specs=[vmem, vmem, smem, smem, smem, smem, smem, pl.BlockSpec(memory_space=pl.ANY), vmem, vmem, smem],
        out_specs=(vmem, vmem, vmem),
        scratch_shapes=scratch,
        compiler_params=pltpu.CompilerParams(
            collective_id=0, has_side_effects=True, vmem_limit_bytes=40 * 1024 * 1024
        ),
    )(
        increment.reshape(tl, cols, lat),
        coeffs,
        polar_rows,
        polar_weight,
        block_index,
        send_dest,
        slot_count,
        jacobian.reshape(n, CAP, obs, lat),
        observed,
        obs_weight,
        bg_weight,
    )
    return gradient.reshape(increment.shape), model_state.reshape(increment.shape), residual


def solution(mesh):
    placed = (
        P(None, None, ("ens", "lon"), None),
        P(None, None, ("ens", "lon"), None),
        P("ens"),
        P("ens"),
        P(("ens", "lon")),
        P(("ens", "lon")),
        P(("ens", "lon")),
        P(("ens", "lon"), None, None),
        P(("ens", "lon"), None),
        P(("ens", "lon"), None),
        P(),
    )
    return jax.shard_map(
        shards,
        mesh=mesh,
        in_specs=placed,
        out_specs=(
            P(None, None, ("ens", "lon"), None),
            P(None, None, ("ens", "lon"), None),
            P(("ens", "lon"), None),
        ),
        check_vma=False,
    )
```

time: 864 us -> 42.8 us (0.05); the launches traced: 854 us -> 42.5 us
  blocking collectives: 485 us -> 0 us
  local copies, waits for them, and re-layouts: 206 us -> 6.28 us
  other arithmetic: 143 us -> 0 us
  Pallas kernels: 0 us -> 35.5 us
  starting transfers between devices: 9.22 us -> 0 us
    psum x8 -> x0, blocking collectives: 485 us -> none  [polar_blend(): zonal_sum = lax.psum(partial_value, 'lon')]
    add x20 -> x0, other arithmetic: 74.8 us -> none  [the longest x3 31 us: retreat_local(): (1.0 - west_c - north_c - south_c) * adjoint_in + from_east + north_in]
    slice x17 -> x0, local copies, waits for them, and re-layouts: 64.2 us -> none  [the longest x7 30.2 us: shards(): west_edge = shifted(model_state[:, :, -1:], 'lon', 1)]
    mul x22 -> x0, other arithmetic: 60.7 us -> none  [the longest x4 27.8 us: retreat_local(): north_flux = north_c * adjoint_in]
    scatter x13 -> x0, local copies, waits for them, and re-layouts: 45.7 us -> none  [the longest x12 44.9 us: polar_blend(): return field_in.at[..., polar_rows].set(blended)]
    pallas_call x0 -> x1, Pallas kernels: none -> 35.5 us  [shards(): pl.pallas_call(functools.partial(kernel, n, sizes), out_shape=(field, fie...]
    gather x8 -> x0, local copies, waits for them, and re-layouts: 23.5 us -> none  [polar_blend(): polar_vals = field_in[..., polar_rows]]
    unnamed x43 -> x25, local copies, waits for them, and re-layouts: 26.1 us -> 6.28 us
  transfers between devices with their start and end apart: 10 -> 0, of which waited for: 1 -> 0; matrix products, arithmetic and copies ran while one was open for 12% -> 0% of each run, Pallas kernels for 0% -> 0%
where the time goes in v1:
time: 42.8 us; the launch traced here: 42.5 us
  Pallas kernels  35.5 us (83%)
  local copies, waits for them, and re-layouts  6.28 us (15%)
  between operations  0.69 us (2%)
    pallas_call x1, Pallas kernels, shards(): pl.pallas_call(functools.partial(kernel, n, sizes), out_shape=(field, fie...  35.5 us
    unnamed x25, local copies, waits for them, and re-layouts  6.28 us

profile of v1, /device:TPU:0, one launch (start us, length us, event | category | flops | bytes accessed | tf_op | source)
XLA Modules:
  0.0 42.5 jit_solution(13891899697987375533)
XLA Ops:
  0.6 0.0 copy-start.9
  0.6 0.8 %copy.14.obs_ref = f32[32,8]{1,0:T(8,128)S(1)} copy(f32[32,8]{0,1:T(8,128)} %param.19) | data formatting | bytes 2048 | tf_op args[8]
  1.4 0.0 copy-done.9
  1.4 0.0 copy-start.3
  1.4 0.0 copy-start.4
  1.4 0.0 copy-start.5
  1.4 0.0 copy-start.6
  1.4 0.0 copy-start.7
  1.5 0.0 copy-start.8
  1.5 0.1 copy.15.ow_ref
  1.5 0.6 %copy-done.3 = f32[4,4]{1,0:T(4,128)S(1)} copy-done((f32[4,4]{1,0:T(4,128)S(1)}, f32[4,4]{1,0:T(4,128)}, u32[]{:S(2)}) %copy-start.3) | copy-done | bytes 88
  2.1 0.0 copy-done.4
  2.1 0.0 copy-done.5
  2.1 0.0 copy-done.6
  2.1 0.0 copy-done.7
  2.1 0.0 copy-done.8
  2.1 0.0 copy-start
  2.1 1.0 %copy-done = f32[32,8,512]{2,1,0:T(8,128)S(1)} copy-done((f32[32,8,512]{2,1,0:T(8,128)S(1)}, f32[32,8,512]{2,1,0:T(8,128)}, u32[]{:S(2)}) %copy-start) | copy-done | bytes 524312
  3.2 0.9 %copy-done.1 = f32[4,4,4,512]{3,2,1,0:T(4,128)S(1)} copy-done((f32[4,4,4,512]{3,2,1,0:T(4,128)S(1)}, f32[4,4,4,512]{3,2,1,0:T(4,128)}, u32[]{:S(2)}) %copy-start.1) | copy-done | bytes 131096
  4.1 0.9 %copy-done.2 = f32[3,4,4,512]{3,2,1,0:T(4,128)S(1)} copy-done((f32[3,4,4,512]{3,2,1,0:T(4,128)S(1)}, f32[3,4,4,512]{3,2,1,0:T(4,128)}, u32[]{:S(2)}) %copy-start.2) | copy-done | bytes 98328
  5.0 35.5 %shard_map.130 = (f32[16,4,512]{2,1,0:T(4,128)S(1)}, f32[16,4,512]{2,1,0:T(4,128)S(1)}, f32[32,8]{1,0:T(8,128)S(1)}) custom-call(f32[16,4,512]{2,1,0:T(4,128)S(1)} %bitcast.7, f32[3,4,4,512]{3,2,1,0:T(4,128)S(1)} %copy-done.2, s32[32]{0:T(128)S(1)} %copy-done.4, f32[32]{0:T(128)S(1)} %copy-done.5, s32[16]{0:T(128)S(1)} %copy-done.6, s32[16]{0:T(128)S(1)} %copy-done.7, ...), custom_call_target="tpu_custom_call" | custom-call | tf_op jit(solution)/shard_map/pallas_call | solution.py:452
  40.5 0.7 %copy.16 = f32[32,8]{0,1:T(8,128)} copy(f32[32,8]{1,0:T(8,128)S(1)} %get-tuple-element.11) | data formatting | bytes 2048
  41.2 0.7 %copy.19 = f32[4,4,4,512]{3,2,1,0:T(4,128)} copy(f32[4,4,4,512]{3,2,1,0:T(4,128)S(1)} %bitcast.6) | data formatting | bytes 262144
  41.8 0.7 %copy.20 = f32[4,4,4,512]{3,2,1,0:T(4,128)} copy(f32[4,4,4,512]{3,2,1,0:T(4,128)S(1)} %bitcast.5) | data formatting | bytes 262144
  (2 shorter events, 0.0 us)
Async XLA Ops:
  0.6 0.8 %copy-start.9 = (f32[32,8]{0,1:T(8,128)S(1)}, f32[32,8]{0,1:T(8,128)}, u32[]{:S(2)}) copy-start(f32[32,8]{0,1:T(8,128)} %param.20) | copy-start | bytes 3076
  1.4 0.7 %copy-start.3 = (f32[4,4]{1,0:T(4,128)S(1)}, f32[4,4]{1,0:T(4,128)}, u32[]{:S(2)}) copy-start(f32[4,4]{1,0:T(4,128)} %bg_ref.1) | copy-start | bytes 196
  1.4 0.7 %copy-start.4 = (s32[32]{0:T(128)S(1)}, s32[32]{0:T(128)}, u32[]{:S(2)}) copy-start(s32[32]{0:T(128)} %rows_ref.1) | copy-start | bytes 388
  1.4 0.7 %copy-start.5 = (f32[32]{0:T(128)S(1)}, f32[32]{0:T(128)}, u32[]{:S(2)}) copy-start(f32[32]{0:T(128)} %pw_ref.1) | copy-start | bytes 388
  1.4 0.7 %copy-start.6 = (s32[16]{0:T(128)S(1)}, s32[16]{0:T(128)}, u32[]{:S(2)}) copy-start(s32[16]{0:T(128)} %bi_ref.1) | copy-start | bytes 196
  1.4 0.7 %copy-start.7 = (s32[16]{0:T(128)S(1)}, s32[16]{0:T(128)}, u32[]{:S(2)}) copy-start(s32[16]{0:T(128)} %sd_ref.1) | copy-start | bytes 196
  1.5 0.7 %copy-start.8 = (s32[16]{0:T(128)S(1)}, s32[16]{0:T(128)}, u32[]{:S(2)}) copy-start(s32[16]{0:T(128)} %sc_ref.1) | copy-start | bytes 196
  2.1 1.0 %copy-start = (f32[32,8,512]{2,1,0:T(8,128)S(1)}, f32[32,8,512]{2,1,0:T(8,128)}, u32[]{:S(2)}) copy-start(f32[32,8,512]{2,1,0:T(8,128)} %param.18) | copy-start | bytes 1572868
  3.2 0.9 %copy-start.1 = (f32[4,4,4,512]{3,2,1,0:T(4,128)S(1)}, f32[4,4,4,512]{3,2,1,0:T(4,128)}, u32[]{:S(2)}) copy-start(f32[4,4,4,512]{3,2,1,0:T(4,128)} %param.11) | copy-start | bytes 393220
  4.1 0.9 %copy-start.2 = (f32[3,4,4,512]{3,2,1,0:T(4,128)S(1)}, f32[3,4,4,512]{3,2,1,0:T(4,128)}, u32[]{:S(2)}) copy-start(f32[3,4,4,512]{3,2,1,0:T(4,128)} %c_ref.1) | copy-start | bytes 294916

commit v2 on v1

v2 whole, which is shorter than its diff:
```python
import functools

import jax
import jax.numpy as jnp
from jax import lax
from jax.experimental import pallas as pl
from jax.experimental.pallas import tpu as pltpu
from jax.sharding import PartitionSpec as P

STEPS = 4
CAP = 2
LANES = 128
HALF = 64
MESH = pl.DeviceIdType.MESH
EXACT = lax.Precision.HIGHEST


def kernel(
    n,
    sizes,
    x_hbm,
    c_hbm,
    rows_hbm,
    pw_hbm,
    bi_hbm,
    sd_hbm,
    sc_hbm,
    jac_hbm,
    obs_hbm,
    ow_hbm,
    bg_hbm,
    grad_ref,
    ms_ref,
    res_ref,
    x_ref,
    c_ref,
    rows_ref,
    pw_ref,
    bi_ref,
    sd_ref,
    sc_ref,
    jac,
    obs_ref,
    ow_ref,
    bg_ref,
    xarr,
    xwest,
    cwest,
    ceast,
    coef,
    msg,
    pbuf,
    pcoef,
    mout,
    mbuf,
    xfin,
    blk_out,
    blk_in,
    ret_out,
    ret_in,
    garr,
    geast,
    gmsg,
    gbuf,
    amout,
    ambuf,
    send_sem,
    recv_sem,
    load_sem,
):
    tl, cols, lat, levels, sends, poles, obs = sizes
    tracers = tl // levels
    spacing = n // levels
    me = lax.axis_index("lon")
    east, west = lax.rem(me + 1, n), lax.rem(me + n - 1, n)

    def others(act):
        def body(k, carry):
            act(lax.rem(me + k, n))
            return carry

        lax.fori_loop(1, n, body, 0, unroll=n <= 16)

    def to_solvers(act):
        for level in range(levels):
            @pl.when(me != level * spacing)
            def _():
                act(level, level * spacing)

    def remote(src, dst, phase, device):
        return pltpu.make_async_remote_copy(
            src_ref=src,
            dst_ref=dst,
            send_sem=send_sem.at[phase],
            recv_sem=recv_sem.at[phase],
            device_id={"lon": device},
            device_id_type=MESH,
        )

    def wait_bytes(ref, sem):
        pltpu.make_async_copy(ref, ref, sem).wait()

    solver = lax.rem(me, spacing) == 0
    level_here = lax.div(me, spacing)

    def wait_solver_blocks(ref, sem):
        @pl.when(solver)
        def _():
            wait_bytes(ref.at[pl.ds(0, levels - 1)], sem)

        @pl.when(jnp.logical_not(solver))
        def _():
            wait_bytes(ref, sem)

    pairs = (
        (x_hbm, x_ref),
        (c_hbm, c_ref),
        (rows_hbm, rows_ref),
        (pw_hbm, pw_ref),
        (bi_hbm, bi_ref),
        (sd_hbm, sd_ref),
        (sc_hbm, sc_ref),
        (obs_hbm, obs_ref),
        (ow_hbm, ow_ref),
        (bg_hbm, bg_ref),
        (jac_hbm, jac),
    )
    loads = [
        pltpu.make_async_copy(src, dst, load_sem.at[i]) for i, (src, dst) in enumerate(pairs)
    ]
    for load in loads:
        load.start()

    barrier = pltpu.get_barrier_semaphore()
    others(
        lambda j: pl.semaphore_signal(
            barrier, inc=1, device_id={"lon": j}, device_id_type=MESH
        ),
    )

    lane = lax.broadcasted_iota(jnp.int32, (1, LANES), 1)
    south = lane < HALF

    def pack(first, last):
        return jnp.where(south, first, last)

    loads[0].wait()
    for t in range(tracers):
        msg[:, t * cols : (t + 1) * cols, :] = pack(
            x_ref[t, :, :, 0:LANES], x_ref[t, :, :, lat - LANES : lat]
        )
    loads[1].wait()
    for kind in range(3):
        lo = (tracers + kind) * cols
        msg[:, lo : lo + cols, :] = pack(
            c_ref[kind, :, :, 0:LANES], c_ref[kind, :, :, lat - LANES : lat]
        )

    pl.semaphore_wait(barrier, n - 1)
    to_solvers(lambda level, j: remote(msg.at[level], pbuf.at[me], 0, j).start())

    for c in range(cols):
        for t in range(tracers):
            lo = c * tl + t * levels
            xarr[lo : lo + levels, :] = x_ref[t, :, c, :]
    to_east = remote(xarr, xwest, 6, east)
    to_east.start()
    coef_east = remote(c_ref, cwest, 7, east)
    coef_east.start()

    @pl.when(solver)
    def _():
        pbuf[pl.ds(me, 1)] = msg[pl.ds(level_here, 1)]

    loads[2].wait()
    loads[3].wait()

    lat_row = lax.broadcasted_iota(jnp.int32, (1, lat), 1)
    weight = jnp.zeros((1, lat), jnp.float32)
    for p in range(poles):
        weight = jnp.where(lat_row == rows_ref[p], pw_ref[p], weight)
    w_first, w_last = weight[:, 0:LANES], weight[:, lat - LANES : lat]
    w_pack = pack(w_first, w_last)
    keep_pack = 1.0 - w_pack

    def edge_free(cn, cs, row, last):
        return jnp.where(row == last, 0.0, cn), jnp.where(row == 0, 0.0, cs)

    def arrange(src, base):
        for c in range(cols):
            cw, cn, cs = src[0, :, c, :], src[1, :, c, :], src[2, :, c, :]
            centre = 1.0 - cw - cn - cs
            cn, cs = edge_free(cn, cs, lat_row, lat - 1)
            for kind, value in enumerate((centre, cw, cn, cs)):
                coef[base + c, kind] = jnp.concatenate([value, value], axis=0)

    def routing(shape, owner_axis):
        owner = lax.broadcasted_iota(jnp.int32, shape, owner_axis)
        block = lax.broadcasted_iota(jnp.int32, shape, 1 - owner_axis)

        def body(k, carry):
            seen, first, second = carry
            index = bi_ref[k]
            row = lax.rem(index, cols) * tl + lax.div(index, cols)
            to_owner = owner == sd_ref[k]
            here = jnp.logical_and(to_owner, block == row)
            first = jnp.where(jnp.logical_and(here, seen == 0), 1.0, first)
            second = jnp.where(jnp.logical_and(here, seen == 1), 1.0, second)
            return jnp.where(to_owner, seen + 1, seen), first, second

        zero = jnp.zeros(shape, jnp.float32)
        init = (jnp.zeros(shape, jnp.int32), zero, zero)
        return lax.fori_loop(0, sends, body, init, unroll=sends <= 16)[1:]

    @pl.when(solver)
    def _():
        wait_bytes(pbuf.at[pl.ds(0, n - 1)], recv_sem.at[0])
        v = [[pbuf[:, t * cols + c, :] for c in range(cols)] for t in range(tracers)]
        packs = []
        for c in range(cols):
            cw, cn, cs = (pbuf[:, (tracers + k) * cols + c, :] for k in range(3))
            centre = 1.0 - cw - cn - cs
            cn, cs = edge_free(cn, cs, lane, LANES - 1)
            packs.append((centre, cw, cn, cs))
            for kind, value in enumerate(packs[c]):
                pcoef[c, kind] = value
        for step in range(STEPS):
            for t in range(tracers):
                new = []
                for c in range(cols):
                    centre, cw, cn, cs = packs[c]
                    from_west = pltpu.roll(v[t][cols - 1], 1, 0) if c == 0 else v[t][c - 1]
                    new.append(
                        centre * v[t][c]
                        + cw * from_west
                        + cn * pltpu.roll(v[t][c], LANES - 1, 1)
                        + cs * pltpu.roll(v[t][c], 1, 1)
                    )
                total = sum(new[1:], new[0])
                mean = jnp.sum(total, axis=0, keepdims=True) / (cols * n)
                row = step * tracers + t
                mout[row : row + 1, :] = mean
                v[t] = [keep_pack * value + w_pack * mean for value in new]
        mbuf[pl.ds(level_here, 1)] = mout[...][None]
        others(lambda j: remote(mout, mbuf.at[level_here], 1, j).start())

    coef_west = remote(c_ref, ceast, 8, west)
    coef_west.start()
    arrange(c_ref, cols)
    loads[4].wait()
    loads[5].wait()
    gather_hot = routing((n, cols * tl), 0)
    coef_east.wait_recv()
    arrange(cwest, 0)
    to_east.wait_recv()
    wait_solver_blocks(mbuf, recv_sem.at[1])

    def means(buf, h, step):
        first = step * tracers + h * 2
        return jnp.concatenate([buf[:, first, :], buf[:, first + 1, :]], axis=0)

    def blend(value, first_mean, last_mean):
        middle = value[:, LANES : lat - LANES]
        first, last = value[:, 0:LANES], value[:, lat - LANES : lat]
        first = (1.0 - w_first) * first + w_first * first_mean
        last = (1.0 - w_last) * last + w_last * last_mean
        return jnp.concatenate([first, middle, last], axis=1)

    group = 2 * levels
    for h in range(tl // group):
        at = lambda c: slice(c * tl + h * group, c * tl + (h + 1) * group)
        v = [xwest[at(c), :] for c in range(cols)] + [xarr[at(c), :] for c in range(cols)]
        for step in range(STEPS):
            mean = means(mbuf, h, step)
            new = list(v)
            for c in range(step + 1, 2 * cols):
                value = (
                    coef[c, 0] * v[c]
                    + coef[c, 1] * v[c - 1]
                    + coef[c, 2] * pltpu.roll(v[c], lat - 1, 1)
                    + coef[c, 3] * pltpu.roll(v[c], 1, 1)
                )
                new[c] = blend(value, mean, mean)
            v = new
        for c in range(cols):
            xfin[at(c), :] = v[cols + c]
            for i in range(2):
                part = v[cols + c][i * levels : (i + 1) * levels]
                ms_ref[2 * h + i, :, c, :] = part

    for r in range(CAP):
        blk_out[:, r, :] = jnp.dot(
            gather_hot[r], xfin[...], precision=EXACT, preferred_element_type=jnp.float32
        )
    others(lambda j: remote(blk_out.at[j], blk_in.at[me], 2, j).start())
    blk_in[pl.ds(me, 1)] = blk_out[pl.ds(me, 1)]
    slots = CAP * n
    loads[6].wait()
    loads[7].wait()
    loads[8].wait()
    slot_lane = lax.broadcasted_iota(jnp.int32, (1, slots), 1)

    def live_body(d, live):
        mine = lax.div(slot_lane, CAP) == d
        on = (lax.rem(slot_lane, CAP) < sc_ref[d]).astype(jnp.float32)
        return jnp.where(mine, on, live)

    live = lax.fori_loop(
        0, n, live_body, jnp.zeros((1, slots), jnp.float32), unroll=n <= 16
    )
    slot_shape = (slots, 1, slots)
    eye = (
        lax.broadcasted_iota(jnp.int32, slot_shape, 0)
        == lax.broadcasted_iota(jnp.int32, slot_shape, 2)
    ).astype(jnp.float32)

    def upright(flat):
        return jnp.sum(flat[None] * eye, axis=2, keepdims=True)

    weighted = upright(ow_ref[...] * live)
    observed = upright(obs_ref[...])
    weight_sum = 1.0 + jnp.sum(weighted, axis=(0, 1), keepdims=True)
    coef_west.wait_recv()
    arrange(ceast, 2 * cols)
    loads[10].wait()
    wait_bytes(blk_in.at[pl.ds(0, n - 1)], recv_sem.at[2])

    w4 = weighted.reshape(n, CAP, obs, 1)
    o4 = observed.reshape(n, CAP, obs, 1)
    misfit = []
    bias_sum = jnp.zeros((1, 1, 1), jnp.float32)
    for r in range(CAP):
        model = jnp.sum(jac[:, r] * blk_in[:, r : r + 1, :], axis=2, keepdims=True)
        misfit.append(model - o4[:, r])
        bias_sum += jnp.sum(w4[:, r] * misfit[r], axis=(0, 1), keepdims=True)
    bias = bias_sum / weight_sum
    residual = [w4[:, r] * (misfit[r] - bias) for r in range(CAP)]
    for r in range(CAP):
        ret_out[:, r : r + 1, :] = jnp.sum(jac[:, r] * residual[r], axis=1, keepdims=True)
    others(lambda j: remote(ret_out.at[j], ret_in.at[me], 3, j).start())
    ret_in[pl.ds(me, 1)] = ret_out[pl.ds(me, 1)]
    both = jnp.stack(residual, axis=1).reshape(slots, obs, 1)
    res_ref[...] = jnp.sum(both * eye, axis=0)
    scatter_hot = routing((cols * tl, n), 1)
    wait_bytes(ret_in.at[pl.ds(0, n - 1)], recv_sem.at[3])

    start = jnp.dot(
        scatter_hot[0], ret_in[:, 0, :], precision=EXACT, preferred_element_type=jnp.float32
    )
    for r in range(1, CAP):
        start += jnp.dot(
            scatter_hot[r], ret_in[:, r, :], precision=EXACT, preferred_element_type=jnp.float32
        )
    garr[...] = start
    for c in range(cols):
        part = start[c * tl : (c + 1) * tl]
        polar = pack(part[:, 0:LANES], part[:, lat - LANES : lat])
        for t in range(tracers):
            gmsg[:, t * cols + c, :] = polar[t * levels : (t + 1) * levels]
    to_solvers(lambda level, j: remote(gmsg.at[level], gbuf.at[me], 4, j).start())
    to_west = remote(garr, geast, 9, west)
    to_west.start()

    @pl.when(solver)
    def _():
        gbuf[pl.ds(me, 1)] = gmsg[pl.ds(level_here, 1)]
        wait_bytes(gbuf.at[pl.ds(0, n - 1)], recv_sem.at[4])
        g = [[gbuf[:, t * cols + c, :] for c in range(cols)] for t in range(tracers)]
        for step in range(STEPS):
            for t in range(tracers):
                total = sum(g[t][1:], g[t][0])
                mean = jnp.sum(total, axis=0, keepdims=True) / (cols * n)
                row = step * tracers + t
                amout[row : row + 1, :] = mean
                if step == STEPS - 1:
                    continue
                part = [keep_pack * value + w_pack * mean for value in g[t]]
                flux = [pcoef[c, 1] * part[c] for c in range(cols)]
                new = []
                for c in range(cols):
                    from_east = pltpu.roll(flux[0], n - 1, 0) if c == cols - 1 else flux[c + 1]
                    new.append(
                        pcoef[c, 0] * part[c]
                        + from_east
                        + pltpu.roll(pcoef[c, 2] * part[c], 1, 1)
                        + pltpu.roll(pcoef[c, 3] * part[c], LANES - 1, 1)
                    )
                g[t] = new
        ambuf[pl.ds(level_here, 1)] = amout[...][None]
        others(lambda j: remote(amout, ambuf.at[level_here], 5, j).start())

    loads[9].wait()
    to_west.wait_recv()
    wait_solver_blocks(ambuf, recv_sem.at[5])

    group_row = lax.broadcasted_iota(jnp.int32, (group, 1), 0)
    for h in range(tl // group):
        at = lambda c: slice(c * tl + h * group, c * tl + (h + 1) * group)
        g = [garr[at(c), :] for c in range(cols)] + [geast[at(c), :] for c in range(cols)]
        for step in range(STEPS):
            mean = means(ambuf, h, step)
            last = 2 * cols - step
            g = [blend(value, mean, mean) for value in g[:last]]
            new = []
            for c in range(last - 1):
                k = cols + c
                new.append(
                    coef[k, 0] * g[c]
                    + coef[k + 1, 1] * g[c + 1]
                    + pltpu.roll(coef[k, 2] * g[c], 1, 1)
                    + pltpu.roll(coef[k, 3] * g[c], lat - 1, 1)
                )
            g = new
        background = jnp.zeros((group, 1), jnp.float32)
        for i in range(group):
            at_row = h * group + i
            value = bg_ref[at_row // levels, at_row % levels]
            background = jnp.where(group_row == i, value, background)
        for c in range(cols):
            value = background * xarr[at(c), :] + g[c]
            for i in range(2):
                grad_ref[2 * h + i, :, c, :] = value[i * levels : (i + 1) * levels]

    wait_solver_blocks(msg, send_sem.at[0])
    wait_bytes(blk_out.at[pl.ds(0, n - 1)], send_sem.at[2])
    wait_bytes(ret_out.at[pl.ds(0, n - 1)], send_sem.at[3])
    wait_solver_blocks(gmsg, send_sem.at[4])

    @pl.when(solver)
    def _():
        def body(s, carry):
            wait_bytes(mout, send_sem.at[1])
            wait_bytes(amout, send_sem.at[5])
            return carry

        lax.fori_loop(1, n, body, 0)

    to_east.wait_send()
    coef_east.wait_send()
    coef_west.wait_send()
    to_west.wait_send()


def shards(
    increment,
    coeffs,
    polar_rows,
    polar_weight,
    block_index,
    send_dest,
    slot_count,
    jacobian,
    observed,
    obs_weight,
    bg_weight,
):
    tracers, levels, cols, lat = increment.shape
    n = lax.axis_size("lon")
    tl = tracers * levels
    obs = jacobian.shape[1]
    sizes = (tl, cols, lat, levels, send_dest.shape[0], polar_rows.shape[0], obs)
    vmem = pl.BlockSpec(memory_space=pltpu.VMEM)
    hbm = pl.BlockSpec(memory_space=pltpu.HBM)
    f32, i32 = jnp.float32, jnp.int32
    field = jax.ShapeDtypeStruct(increment.shape, f32)
    flat = jax.ShapeDtypeStruct((obs, CAP * n), f32)
    rows = (tracers + 3) * cols
    scratch = [
        pltpu.VMEM(increment.shape, f32),
        pltpu.VMEM(coeffs.shape, f32),
        pltpu.SMEM(polar_rows.shape, i32),
        pltpu.SMEM(polar_weight.shape, f32),
        pltpu.SMEM(block_index.shape, i32),
        pltpu.SMEM(send_dest.shape, i32),
        pltpu.SMEM(slot_count.shape, i32),
        pltpu.VMEM((n, CAP, obs, lat), f32),
        pltpu.VMEM(flat.shape, f32),
        pltpu.VMEM(flat.shape, f32),
        pltpu.SMEM(bg_weight.shape, f32),
        pltpu.VMEM((cols * tl, lat), f32),
        pltpu.VMEM((cols * tl, lat), f32),
        pltpu.VMEM(coeffs.shape, f32),
        pltpu.VMEM(coeffs.shape, f32),
        pltpu.VMEM((3 * cols, 4, 2 * levels, lat), f32),
        pltpu.VMEM((levels, rows, LANES), f32),
        pltpu.VMEM((n, rows, LANES), f32),
        pltpu.VMEM((cols, 4, n, LANES), f32),
        pltpu.VMEM((STEPS * tracers, LANES), f32),
        pltpu.VMEM((levels, STEPS * tracers, LANES), f32),
        pltpu.VMEM((cols * tl, lat), f32),
        pltpu.VMEM((n, CAP, lat), f32),
        pltpu.VMEM((n, CAP, lat), f32),
        pltpu.VMEM((n, CAP, lat), f32),
        pltpu.VMEM((n, CAP, lat), f32),
        pltpu.VMEM((cols * tl, lat), f32),
        pltpu.VMEM((cols * tl, lat), f32),
        pltpu.VMEM((levels, tracers * cols, LANES), f32),
        pltpu.VMEM((n, tracers * cols, LANES), f32),
        pltpu.VMEM((STEPS * tracers, LANES), f32),
        pltpu.VMEM((levels, STEPS * tracers, LANES), f32),
        pltpu.SemaphoreType.DMA((10,)),
        pltpu.SemaphoreType.DMA((10,)),
        pltpu.SemaphoreType.DMA((11,)),
    ]
    gradient, model_state, residual = pl.pallas_call(
        functools.partial(kernel, n, sizes),
        out_shape=(field, field, flat),
        in_specs=[hbm] * 11,
        out_specs=(vmem, vmem, vmem),
        scratch_shapes=scratch,
        compiler_params=pltpu.CompilerParams(
            collective_id=0, has_side_effects=True, vmem_limit_bytes=62 * 1024 * 1024
        ),
    )(
        increment,
        coeffs,
        polar_rows,
        polar_weight,
        block_index,
        send_dest,
        slot_count,
        jacobian.reshape(n, CAP, obs, lat),
        observed.T,
        obs_weight.T,
        bg_weight,
    )
    return gradient, model_state, residual.T


def solution(mesh):
    placed = (
        P(None, None, ("ens", "lon"), None),
        P(None, None, ("ens", "lon"), None),
        P("ens"),
        P("ens"),
        P(("ens", "lon")),
        P(("ens", "lon")),
        P(("ens", "lon")),
        P(("ens", "lon"), None, None),
        P(("ens", "lon"), None),
        P(("ens", "lon"), None),
        P(),
    )
    return jax.shard_map(
        shards,
        mesh=mesh,
        in_specs=placed,
        out_specs=(
            P(None, None, ("ens", "lon"), None),
            P(None, None, ("ens", "lon"), None),
            P(("ens", "lon"), None),
        ),
        check_vma=False,
    )
```

time: 42.8 us -> 39.7 us (0.928)
  local copies, waits for them, and re-layouts: 6.28 us -> 2.88 us
  Pallas kernels: 35.5 us -> 36 us
    unnamed x25 -> x7, local copies, waits for them, and re-layouts: 6.28 us -> 2.88 us
    pallas_call x1, Pallas kernels: 35.5 us -> 36 us  [shards(): pl.pallas_call(functools.partial(kernel, n, sizes), out_shape=(field, fie...]
where the time goes in v2:
time: 39.7 us; the launch traced here: 39.5 us
  Pallas kernels  36 us (91%)
  local copies, waits for them, and re-layouts  2.88 us (7%)
  between operations  0.65 us (2%)
    pallas_call x1, Pallas kernels, shards(): pl.pallas_call(functools.partial(kernel, n, sizes), out_shape=(field, fie...  36 us
    unnamed x7, local copies, waits for them, and re-layouts  2.88 us

profile of v2, /device:TPU:0, one launch (start us, length us, event | category | flops | bytes accessed | tf_op | source)
XLA Modules:
  0.0 39.5 jit_solution(12143260912342404300)
XLA Ops:
  0.6 36.0 %shard_map.130 = (f32[4,4,4,512]{3,2,1,0:T(4,128)}, f32[4,4,4,512]{3,2,1,0:T(4,128)}, f32[8,32]{1,0:T(8,128)}) custom-call(f32[4,4,4,512]{3,2,1,0:T(4,128)} %x_hbm.1, f32[3,4,4,512]{3,2,1,0:T(4,128)} %c_hbm.1, s32[32]{0:T(128)} %rows_hbm.1, f32[32]{0:T(128)} %pw_hbm.1, s32[16]{0:T(128)} %bi_hbm.1, s32[16]{0:T(128)} %sd_hbm.1, s32[16]{0:T(128)} %sc_hbm.1, ...), custom_call_target="tpu_custom_call" | custom-call | tf_op jit(solution)/shard_map/pallas_call | solution.py:505
  36.7 0.0 copy-start
  36.7 1.6 %copy.17 = f32[4,4,4,512]{3,2,1,0:T(4,128)} copy(f32[4,4,4,512]{3,2,1,0:T(4,128)} %get-tuple-element.12) | data formatting | bytes 262144
  38.3 0.0 copy-done
  38.3 0.0 copy-start.1
  38.3 0.7 %copy.18 = f32[4,4,4,512]{3,2,1,0:T(4,128)} copy(f32[4,4,4,512]{3,2,1,0:T(4,128)S(1)} %copy-done) | data formatting | bytes 262144
  38.9 0.0 copy-done.1
  39.0 0.6 %copy.19 = f32[32,8]{0,1:T(8,128)} copy(f32[32,8]{0,1:T(8,128)S(1)} %bitcast.7) | data formatting | bytes 2048
Async XLA Ops:
  36.7 1.6 %copy-start = (f32[4,4,4,512]{3,2,1,0:T(4,128)S(1)}, f32[4,4,4,512]{3,2,1,0:T(4,128)}, u32[]{:S(2)}) copy-start(f32[4,4,4,512]{3,2,1,0:T(4,128)} %get-tuple-element.13) | copy-start | bytes 393220
  38.3 0.7 %copy-start.1 = (f32[8,32]{1,0:T(8,128)S(1)}, f32[8,32]{1,0:T(8,128)}, u32[]{:S(2)}) copy-start(f32[8,32]{1,0:T(8,128)} %get-tuple-element.8) | copy-start | bytes 3076

commit v3 on v2

--- a/solution.py
+++ b/solution.py
@@ -439,6 +439,15 @@
     coef_east.wait_send()
     coef_west.wait_send()
     to_west.wait_send()
+
+
+def store(*refs):
+    sem = refs[6]
+    copies = [pltpu.make_async_copy(refs[i], refs[i + 3], sem.at[i]) for i in range(3)]
+    for copy in copies:
+        copy.start()
+    for copy in copies:
+        copy.wait()
 
 
 def shards(
@@ -524,6 +533,13 @@
         obs_weight.T,
         bg_weight,
     )
+    gradient, model_state, residual = pl.pallas_call(
+        store,
+        out_shape=(field, field, flat),
+        in_specs=[hbm] * 3,
+        out_specs=(vmem, vmem, vmem),
+        scratch_shapes=[pltpu.SemaphoreType.DMA((3,))],
+    )(gradient, model_state, residual)
     return gradient, model_state, residual.T
 
 

time: 39.7 us -> 38.5 us (0.970)
  local copies, waits for them, and re-layouts: 2.88 us -> 0 us
  Pallas kernels: 36 us -> 37.7 us
    unnamed x7 -> x0, local copies, waits for them, and re-layouts: 2.88 us -> none
    pallas_call x0 -> x1, Pallas kernels: none -> 1.7 us  [shards(): pl.pallas_call(store, out_shape=(field, field, flat), in_specs=[hbm] * 3,...]
where the time goes in v3:
time: 38.5 us; the launch traced here: 38.4 us
  Pallas kernels  37.7 us (98%)
  between operations  0.64 us (2%)
    pallas_call x1, Pallas kernels, shards(): pl.pallas_call(functools.partial(kernel, n, sizes), out_shape=(field, fie...  36 us
    pallas_call x1, Pallas kernels, shards(): pl.pallas_call(store, out_shape=(field, field, flat), in_specs=[hbm] * 3,...  1.7 us

profile of v3, /device:TPU:0, one launch (start us, length us, event | category | flops | bytes accessed | tf_op | source)
XLA Modules:
  0.0 38.4 jit_solution(7150710246264149701)
XLA Ops:
  0.6 36.0 %shard_map.130 = (f32[4,4,4,512]{3,2,1,0:T(4,128)}, f32[4,4,4,512]{3,2,1,0:T(4,128)}, f32[8,32]{1,0:T(8,128)}) custom-call(f32[4,4,4,512]{3,2,1,0:T(4,128)} %x_hbm.1, f32[3,4,4,512]{3,2,1,0:T(4,128)} %c_hbm.1, s32[32]{0:T(128)} %rows_hbm.1, f32[32]{0:T(128)} %pw_hbm.1, s32[16]{0:T(128)} %bi_hbm.1, s32[16]{0:T(128)} %sd_hbm.1, s32[16]{0:T(128)} %sc_hbm.1, ...), custom_call_target="tpu_custom_call" | custom-call | tf_op jit(solution)/shard_map/pallas_call | solution.py:514
  36.7 1.7 %shard_map.131 = (f32[4,4,4,512]{3,2,1,0:T(4,128)}, f32[4,4,4,512]{3,2,1,0:T(4,128)}, f32[8,32]{1,0:T(8,128)}) custom-call(f32[4,4,4,512]{3,2,1,0:T(4,128)} %get-tuple-element.9.refs_0_, f32[4,4,4,512]{3,2,1,0:T(4,128)} %get-tuple-element.10.refs_1_, f32[8,32]{1,0:T(8,128)} %get-tuple-element.11.refs_2_), custom_call_target="tpu_custom_call" | custom-call | tf_op jit(solution)/shard_map/pallas_call | solution.py:536

commit v4 on v3

--- a/solution.py
+++ b/solution.py
@@ -70,7 +70,7 @@
 ):
     tl, cols, lat, levels, sends, poles, obs = sizes
     tracers = tl // levels
-    spacing = n // levels
+    spacing, nearest = n // (2 * levels), n // 4
     me = lax.axis_index("lon")
     east, west = lax.rem(me + 1, n), lax.rem(me + n - 1, n)
 
@@ -83,9 +83,9 @@
 
     def to_solvers(act):
         for level in range(levels):
-            @pl.when(me != level * spacing)
+            @pl.when(me != nearest + level * spacing)
             def _():
-                act(level, level * spacing)
+                act(level, nearest + level * spacing)
 
     def remote(src, dst, phase, device):
         return pltpu.make_async_remote_copy(
@@ -100,8 +100,10 @@
     def wait_bytes(ref, sem):
         pltpu.make_async_copy(ref, ref, sem).wait()
 
-    solver = lax.rem(me, spacing) == 0
-    level_here = lax.div(me, spacing)
+    solver = functools.reduce(
+        jnp.logical_or, [me == nearest + level * spacing for level in range(levels)]
+    )
+    level_here = lax.div(me - nearest, spacing)
 
     def wait_solver_blocks(ref, sem):
         @pl.when(solver)

time: 38.5 us -> 36.6 us (0.951)
  Pallas kernels: 37.7 us -> 35.8 us
    pallas_call x1, Pallas kernels: 36 us -> 34.1 us  [shards(): pl.pallas_call(functools.partial(kernel, n, sizes), out_shape=(field, fie...]
where the time goes in v4:
time: 36.6 us; the launch traced here: 36.4 us
  Pallas kernels  35.8 us (98%)
  between operations  0.64 us (2%)
    pallas_call x1, Pallas kernels, shards(): pl.pallas_call(functools.partial(kernel, n, sizes), out_shape=(field, fie...  34.1 us
    pallas_call x1, Pallas kernels, shards(): pl.pallas_call(store, out_shape=(field, field, flat), in_specs=[hbm] * 3,...  1.7 us

profile of v4, /device:TPU:0, one launch (start us, length us, event | category | flops | bytes accessed | tf_op | source)
XLA Modules:
  0.0 36.4 jit_solution(2208602656796884551)
XLA Ops:
  0.6 34.1 %shard_map.130 = (f32[4,4,4,512]{3,2,1,0:T(4,128)}, f32[4,4,4,512]{3,2,1,0:T(4,128)}, f32[8,32]{1,0:T(8,128)}) custom-call(f32[4,4,4,512]{3,2,1,0:T(4,128)} %x_hbm.1, f32[3,4,4,512]{3,2,1,0:T(4,128)} %c_hbm.1, s32[32]{0:T(128)} %rows_hbm.1, f32[32]{0:T(128)} %pw_hbm.1, s32[16]{0:T(128)} %bi_hbm.1, s32[16]{0:T(128)} %sd_hbm.1, s32[16]{0:T(128)} %sc_hbm.1, ...), custom_call_target="tpu_custom_call" | custom-call | tf_op jit(solution)/shard_map/pallas_call | solution.py:516
  34.7 1.7 %shard_map.131 = (f32[4,4,4,512]{3,2,1,0:T(4,128)}, f32[4,4,4,512]{3,2,1,0:T(4,128)}, f32[8,32]{1,0:T(8,128)}) custom-call(f32[4,4,4,512]{3,2,1,0:T(4,128)} %get-tuple-element.9.refs_0_, f32[4,4,4,512]{3,2,1,0:T(4,128)} %get-tuple-element.10.refs_1_, f32[8,32]{1,0:T(8,128)} %get-tuple-element.11.refs_2_), custom_call_target="tpu_custom_call" | custom-call | tf_op jit(solution)/shard_map/pallas_call | solution.py:538
